TPU v7x, 32 devices: a whole 2x2x4 slice. The times are simulated.
32 devices in a mesh: grp: 2 (over x), ang: 2 (over core), zs: 8 (over z, y).
Axes of the slice: x: 2, y: 2, z: 4, core: 2. Of those that a mesh axis runs over, the one named last changes fastest.
Arguments:
- projections: bfloat16 [256, 256, 4096], P(('grp', 'ang', 'zs')), parts along dimension 0, may hold values from 0 to 6
- view_angle: float32 [256], P(('grp', 'ang', 'zs')), parts along dimension 0, may hold values from 0 to 4.14
- band_offset: int32 [256, 8], P(('grp', 'ang', 'zs')), parts along dimension 0, may hold values from 0 to 224
- band_count: int32 [256, 8], P(('grp', 'ang', 'zs')), parts along dimension 0, may hold values from 0 to 32, as said below
- fp_start: int32 [256], P(('grp', 'ang', 'zs')), parts along dimension 0, may hold values from 0 to 3072
- footprint: bfloat16 [256, 1024, 128], P(('grp', 'ang')), parts along dimension 0, may hold values from -0.75 to 0.75
Outputs:
- volume: float32 [512, 128], P(('grp', 'zs'), 'ang'), parts along dimension 0
There are 2 independent parts, one for each index of `grp`. A program takes and returns all parts, laid end to end along the dimension named above; each array names one. Nothing has to cross between parts.
Inputs may be any that keep to these rules, and one draw needn't show every extreme that they name: `band_count`: counts reach 32 in every draw.
All inputs are finite; a program needn't handle non-finite values.
Results may differ from a plain program's by a relative error of at most 0.00035.
The roundings to bfloat16 on the way count: a program that leaves them out, or rounds other values in their place, can miss the bound.
Values may be sent and summed in bfloat16 or wider, within the bound.
A program may use at most 192 MiB of HBM per device.

v0:
```python
import math

import jax
import jax.numpy as jnp
from jax import lax
from jax.sharding import PartitionSpec as P

BAND = 32


fan_half = 0.5


def parker_weight(beta, columns):
    column_pos = jnp.arange(columns).astype(jnp.float32)
    gamma = fan_half * ((2.0 * column_pos + 1.0) / columns - 1.0)
    rising = jnp.sin(math.pi / 4.0 * beta / (fan_half - gamma)) ** 2
    falling = jnp.sin(math.pi / 4.0 * (math.pi + 2.0 * fan_half - beta) / (fan_half + gamma)) ** 2
    parker = jnp.where(
        beta < 2.0 * (fan_half - gamma),
        rising,
        jnp.where(beta > math.pi - 2.0 * gamma, falling, 1.0),
    )
    return parker * jnp.cos(gamma)


def ramp_table(first_col, columns, width):
    offsets = jnp.arange(columns)[:, None] - first_col - jnp.arange(width)[None, :]
    offset_real = offsets.astype(jnp.float32)
    is_odd = jnp.abs(offsets) % 2 == 1
    values = jnp.where(
        offsets == 0,
        0.25,
        jnp.where(is_odd, -1.0 / (math.pi**2 * jnp.maximum(offset_real * offset_real, 1.0)), 0.0),
    )
    return values.astype(jnp.bfloat16)


def shards(projections, view_angle, band_offset, band_count, fp_start, footprint):
    columns = projections.shape[2]
    width = footprint.shape[1]
    band_rows = BAND

    def filter_view(packed):
        view_rows, beta, first_col = packed
        weight = parker_weight(beta, columns)
        weighted = (view_rows * weight[None, :]).astype(jnp.bfloat16)
        kernel = ramp_table(first_col, columns, width)
        return jnp.dot(weighted, kernel, preferred_element_type=jnp.float32).astype(jnp.bfloat16)

    filtered = lax.map(filter_view, (projections, view_angle, fp_start))

    def cut_band(view_filtered, first_row, row_count):
        rows_taken = lax.dynamic_slice_in_dim(view_filtered, first_row, band_rows, 0)
        keep_rows = jnp.arange(band_rows) < row_count
        return jnp.where(keep_rows[:, None], rows_taken, jnp.zeros_like(rows_taken))

    bands = jax.vmap(jax.vmap(cut_band, in_axes=(0, 0, 0)), in_axes=(None, 1, 1))(
        filtered, band_offset, band_count
    )
    received = lax.all_to_all(bands, "zs", split_axis=0, concat_axis=0, tiled=True)
    received = received.reshape(-1, band_rows, width)
    slab_part = jnp.einsum("apc,acv->pv", received, footprint, preferred_element_type=jnp.float32)
    return lax.psum_scatter(slab_part, "ang", scatter_dimension=1, tiled=True)


def solution(mesh):
    in_specs = (
        P(("grp", "ang", "zs"), None, None),
        P(("grp", "ang", "zs")),
        P(("grp", "ang", "zs"), None),
        P(("grp", "ang", "zs"), None),
        P(("grp", "ang", "zs")),
        P(("grp", "ang"), None, None),
    )
    out_specs = P(("grp", "zs"), "ang")
    return jax.shard_map(shards, mesh=mesh, in_specs=in_specs, out_specs=out_specs, check_vma=False)
```

profile of v0, /device:TPU:0, one launch (start us, length us, event | category | flops | bytes accessed | tf_op | source)
XLA Modules:
  0.0 342.9 jit_solution(8408203359809001537)
XLA Ops:
  6.5 183.3 %while.12 = (s32[]{:T(128)}, bf16[8,256,1024]{2,1,0:T(8,128)(2,1)}, bf16[8,256,4096]{2,1,0:T(8,128)(2,1)}, f32[8]{0:T(128)}, s32[8]{0:T(128)}, /*index=5*/s32[]{:T(128)}, f32[]{:T(128)}, f32[]{:T(128)}) while((s32[]{:T(128)}, bf16[8,256,1024]{2,1,0:T(8,128)(2,1)}, bf16[8,256,4096]{2,1,0:T(8,128)(2,1)}, f32[8]{0:T(128)}, s32[8]{0:T(128)}, ...), condition=%wide.region_1.2_spmd, body=%wide.region_0.1_spmd.sunk | while | flops 2247442432 | bytes 2688161 | solution.py:51
  6.5 1.3 dynamic_slice.36
  9.8 1.3 dynamic_slice.35
  11.7 17.7 %fusion.35 = bf16[8,256,1024]{2,1,0:T(8,128)(2,1)} fusion(bf16[8,256,1024]{2,1,0:T(8,128)(2,1)} %get-tuple-element.124, s32[]{:T(128)} %get-tuple-element.123, s32[4096]{0:T(1024)S(1)} %iota_subtract_fusion.3, f32[4096]{0:T(1024)S(1)} %cosine_multiply_fusion.2, bf16[8,256,4096]{2,1,0:T(8,128)(2,1)} %get-tuple-element.133), kind=kOutput, calls=%fused_computation.17.clone.1 | convolution fusion | flops 2247360512 | bytes 2655232 | tf_op jit(solution)/shard_map/while/body/eval_jaxpr/dot_general | solution.py:49
  29.4 1.3 dynamic_slice.36
  32.7 1.3 dynamic_slice.35
  34.6 17.7 %fusion.35 = bf16[8,256,1024]{2,1,0:T(8,128)(2,1)} fusion(bf16[8,256,1024]{2,1,0:T(8,128)(2,1)} %get-tuple-element.124, s32[]{:T(128)} %get-tuple-element.123, s32[4096]{0:T(1024)S(1)} %iota_subtract_fusion.3, f32[4096]{0:T(1024)S(1)} %cosine_multiply_fusion.2, bf16[8,256,4096]{2,1,0:T(8,128)(2,1)} %get-tuple-element.133), kind=kOutput, calls=%fused_computation.17.clone.1 | convolution fusion | flops 2247360512 | bytes 2655232 | tf_op jit(solution)/shard_map/while/body/eval_jaxpr/dot_general | solution.py:49
  52.4 1.3 dynamic_slice.36
  55.6 1.3 dynamic_slice.35
  57.5 17.7 %fusion.35 = bf16[8,256,1024]{2,1,0:T(8,128)(2,1)} fusion(bf16[8,256,1024]{2,1,0:T(8,128)(2,1)} %get-tuple-element.124, s32[]{:T(128)} %get-tuple-element.123, s32[4096]{0:T(1024)S(1)} %iota_subtract_fusion.3, f32[4096]{0:T(1024)S(1)} %cosine_multiply_fusion.2, bf16[8,256,4096]{2,1,0:T(8,128)(2,1)} %get-tuple-element.133), kind=kOutput, calls=%fused_computation.17.clone.1 | convolution fusion | flops 2247360512 | bytes 2655232 | tf_op jit(solution)/shard_map/while/body/eval_jaxpr/dot_general | solution.py:49
  75.3 1.3 dynamic_slice.36
  78.6 1.3 dynamic_slice.35
  80.5 17.7 %fusion.35 = bf16[8,256,1024]{2,1,0:T(8,128)(2,1)} fusion(bf16[8,256,1024]{2,1,0:T(8,128)(2,1)} %get-tuple-element.124, s32[]{:T(128)} %get-tuple-element.123, s32[4096]{0:T(1024)S(1)} %iota_subtract_fusion.3, f32[4096]{0:T(1024)S(1)} %cosine_multiply_fusion.2, bf16[8,256,4096]{2,1,0:T(8,128)(2,1)} %get-tuple-element.133), kind=kOutput, calls=%fused_computation.17.clone.1 | convolution fusion | flops 2247360512 | bytes 2655232 | tf_op jit(solution)/shard_map/while/body/eval_jaxpr/dot_general | solution.py:49
  98.2 1.3 dynamic_slice.36
  101.5 1.3 dynamic_slice.35
  103.4 17.7 %fusion.35 = bf16[8,256,1024]{2,1,0:T(8,128)(2,1)} fusion(bf16[8,256,1024]{2,1,0:T(8,128)(2,1)} %get-tuple-element.124, s32[]{:T(128)} %get-tuple-element.123, s32[4096]{0:T(1024)S(1)} %iota_subtract_fusion.3, f32[4096]{0:T(1024)S(1)} %cosine_multiply_fusion.2, bf16[8,256,4096]{2,1,0:T(8,128)(2,1)} %get-tuple-element.133), kind=kOutput, calls=%fused_computation.17.clone.1 | convolution fusion | flops 2247360512 | bytes 2655232 | tf_op jit(solution)/shard_map/while/body/eval_jaxpr/dot_general | solution.py:49
  121.1 1.3 dynamic_slice.36
  124.4 1.3 dynamic_slice.35
  126.3 17.7 %fusion.35 = bf16[8,256,1024]{2,1,0:T(8,128)(2,1)} fusion(bf16[8,256,1024]{2,1,0:T(8,128)(2,1)} %get-tuple-element.124, s32[]{:T(128)} %get-tuple-element.123, s32[4096]{0:T(1024)S(1)} %iota_subtract_fusion.3, f32[4096]{0:T(1024)S(1)} %cosine_multiply_fusion.2, bf16[8,256,4096]{2,1,0:T(8,128)(2,1)} %get-tuple-element.133), kind=kOutput, calls=%fused_computation.17.clone.1 | convolution fusion | flops 2247360512 | bytes 2655232 | tf_op jit(solution)/shard_map/while/body/eval_jaxpr/dot_general | solution.py:49
  144.0 1.3 dynamic_slice.36
  147.3 1.3 dynamic_slice.35
  149.2 17.7 %fusion.35 = bf16[8,256,1024]{2,1,0:T(8,128)(2,1)} fusion(bf16[8,256,1024]{2,1,0:T(8,128)(2,1)} %get-tuple-element.124, s32[]{:T(128)} %get-tuple-element.123, s32[4096]{0:T(1024)S(1)} %iota_subtract_fusion.3, f32[4096]{0:T(1024)S(1)} %cosine_multiply_fusion.2, bf16[8,256,4096]{2,1,0:T(8,128)(2,1)} %get-tuple-element.133), kind=kOutput, calls=%fused_computation.17.clone.1 | convolution fusion | flops 2247360512 | bytes 2655232 | tf_op jit(solution)/shard_map/while/body/eval_jaxpr/dot_general | solution.py:49
  166.9 1.3 dynamic_slice.36
  170.2 1.3 dynamic_slice.35
  172.0 17.8 %fusion.35 = bf16[8,256,1024]{2,1,0:T(8,128)(2,1)} fusion(bf16[8,256,1024]{2,1,0:T(8,128)(2,1)} %get-tuple-element.124, s32[]{:T(128)} %get-tuple-element.123, s32[4096]{0:T(1024)S(1)} %iota_subtract_fusion.3, f32[4096]{0:T(1024)S(1)} %cosine_multiply_fusion.2, bf16[8,256,4096]{2,1,0:T(8,128)(2,1)} %get-tuple-element.133), kind=kOutput, calls=%fused_computation.17.clone.1 | convolution fusion | flops 2247360512 | bytes 2655232 | tf_op jit(solution)/shard_map/while/body/eval_jaxpr/dot_general | solution.py:49
  189.8 6.5 %copy.17 = bf16[8,256,1024]{2,0,1:T(8,128)(2,1)} copy(bf16[8,256,1024]{2,1,0:T(8,128)(2,1)} %get-tuple-element.73) | data formatting | bytes 8388608 | tf_op jit(solution)/shard_map/while | solution.py:51
  196.6 12.5 %gather_fusion = bf16[64,32,1024]{2,0,1:T(8,128)(2,1)} fusion(bf16[8,256,1024]{2,0,1:T(8,128)(2,1)} %copy.17, s32[64]{0:T(128)S(1)} %reshape.43), kind=kCustom, calls=%fused_computation | custom fusion | bytes 8389376 | tf_op jit(solution)/shard_map/vmap(vmap())/gather | solution.py:54
  209.1 8.1 %copy_select_fusion = bf16[8,8,32,1024]{3,2,1,0:T(8,128)(2,1)S(1)} fusion(bf16[8,8,32,1024]{3,1,0,2:T(8,128)(2,1)} %bitcast.46, pred[8,8,32]{2,1,0:T(8,128)(4,1)S(1)} %iota_compare_fusion), kind=kLoop, calls=%fused_computation.31 | loop fusion | flops 2097152 | bytes 8390656 | tf_op jit(solution)/shard_map/vmap(vmap(jit(_where)))/select_n | solution.py:56
  217.2 100.1 %all_to_all.5 = bf16[8,8,32,1024]{3,2,1,0:T(8,128)(2,1)S(1)} all-to-all(bf16[8,8,32,1024]{3,2,1,0:T(8,128)(2,1)S(1)} %copy_select_fusion), channel_id=1, replica_groups=mesh['grp'=2,'ang'=2,'zs'=8] {'zs'}, dimensions={0} | all-to-all | bytes 8388608 | tf_op jit(solution)/shard_map/all_to_all | solution.py:61
  317.3 10.8 %convolution_bitcast_fusion = f32[128,32]{1,0:T(8,128)} fusion(bf16[64,32,1024]{2,1,0:T(8,128)(2,1)S(1)} %bitcast.45, bf16[64,1024,128]{2,1,0:T(8,128)(2,1)} %param.13), kind=kOutput, calls=%fused_computation.32 | convolution fusion | flops 536870912 | bytes 20987904 | tf_op jit(solution)/shard_map/apc,acv->pv/dot_general | solution.py:63
  328.1 6.5 %reduce-scatter.4.cloned.1.call-done = f32[64,32]{1,0:T(8,128)} async-done(((f32[128,32]{1,0:T(8,128)}), f32[64,32]{1,0:T(8,128)}) %reduce-scatter.4.cloned.1.call-update) | async-done | bytes 8208
  334.6 1.4 copy.20
  (28 shorter events, 11.6 us)
Async XLA Ops:
  6.5 328.1 %reduce-scatter.4.cloned.1.call-start = ((), (), s32[]{:S(2)}) async-start(), calls=%async_computation.2 | async-start | bytes 98304
  189.8 6.5 %copy-start = (s32[8,8]{1,0:T(8,128)S(1)}, s32[8,8]{1,0:T(8,128)}, u32[]{:S(2)}) copy-start(s32[8,8]{1,0:T(8,128)} %param.10) | copy-start | bytes 772
  189.8 6.6 %copy-start.1 = (s32[8,8]{1,0:T(8,128)S(1)}, s32[8,8]{1,0:T(8,128)}, u32[]{:S(2)}) copy-start(s32[8,8]{1,0:T(8,128)} %param.11) | copy-start | bytes 772
Sparse Core Ops, SparseCore 0:
  328.2 6.3 reduce-scatter.3
where the time goes:
time: 344 us; the launch traced here: 343 us
  matrix products  153 us (44%)
  blocking collectives  100 us (29%)
  local copies, waits for them, and re-layouts  41 us (12%)
  other arithmetic  19.4 us (6%)
  between operations  13.4 us (4%)
  loops' own time  9.86 us (3%)
  waiting for transfers between devices  6.53 us (2%)
    dot_general x8, matrix products, filter_view(): jnp.dot(weighted, kernel, preferred_element_type=jnp.float32)  142 us
    all_to_all x1, blocking collectives, shards(): lax.all_to_all(bands, 'zs', split_axis=0, concat_axis=0, tiled=True)  100 us
    dynamic_slice x16, local copies, waits for them, and re-layouts, shards(): filtered = lax.map(filter_view, (projections, view_angle, fp_start))  20.3 us
    gather x2, local copies, waits for them, and re-layouts, cut_band(): lax.dynamic_slice_in_dim(view_filtered, first_row, band_rows, 0)  12.6 us
    dot_general x1, matrix products, shards(): jnp.einsum('apc,acv->pv', received, footprint, preferred_element_type=jnp...  10.8 us
    another operation x1, loops' own time, shards(): filtered = lax.map(filter_view, (projections, view_angle, fp_start))  9.86 us
    select_n x1, other arithmetic, cut_band(): return jnp.where(keep_rows[:, None], rows_taken, jnp.zeros_like(rows_taken))  8.06 us
  transfers between devices with their start and end apart: 1, of which 1 were waited for; matrix products, arithmetic and copies ran while one was open for 0% of the time, Pallas kernels for 0%

commit v1 on v0

v1 whole, which is shorter than its diff:
```python
import functools
import math

import jax
import jax.numpy as jnp
from jax import lax
from jax.experimental import pallas as pl
from jax.experimental.pallas import tpu as pltpu
from jax.sharding import PartitionSpec as P

BAND = 32
FAN_HALF = 0.5
LANES = 128
ALIGN = 32
KC = 512
F32 = jnp.float32
BF16 = jnp.bfloat16
NT = (((1,), (1,)), ((), ()))
TN = (((0,), (0,)), ((), ()))


def fan_weight(beta, columns):
    shape = (beta.shape[0], columns)
    position = lax.broadcasted_iota(jnp.int32, shape, 1).astype(F32)
    gamma = FAN_HALF * ((2.0 * position + 1.0) / columns - 1.0)
    rising = math.pi / 4.0 * beta / (FAN_HALF - gamma)
    falling = math.pi / 4.0 * (math.pi + 2.0 * FAN_HALF - beta) / (FAN_HALF + gamma)
    flat = jnp.full(shape, math.pi / 2.0, F32)
    angle = jnp.where(
        beta < 2.0 * (FAN_HALF - gamma),
        rising,
        jnp.where(beta > math.pi - 2.0 * gamma, falling, flat),
    )
    return jnp.sin(angle) ** 2 * jnp.cos(gamma)


def odd_ramp(offsets):
    real = offsets.astype(F32)
    return (-1.0 / (math.pi**2 * (real * real))).astype(BF16)


def kernel(
    sizes,
    start_ref, offset_ref, count_ref, angle_ref, proj_ref, foot_ref, out_ref,
    proj_buf, foot_buf, foot_wide, weight, pick, ramp_even, ramp_odd,
    w_even, w_odd, diag_even, diag_odd, grid_rows, volume, proj_sem, foot_sem,
):
    n_zs, n_ang, views, columns, width = sizes
    half = columns // 2
    window = (width + ALIGN) // 2
    my_zs = lax.axis_index("zs")

    def proj_copy(view, slot):
        return pltpu.make_async_copy(proj_ref.at[view], proj_buf.at[slot], proj_sem.at[slot])

    proj_copy(0, 0).start()
    proj_copy(1, 1).start()
    foot_copy = pltpu.make_async_copy(
        foot_ref.at[pl.ds(my_zs * views, views)], foot_buf, foot_sem
    )
    foot_copy.start()

    weight[...] = fan_weight(angle_ref[...], columns)

    row = lax.broadcasted_iota(jnp.int32, (256, 256), 0)
    col = lax.broadcasted_iota(jnp.int32, (256, 256), 1)
    source = jnp.where(col < LANES, 2 * col, 2 * (col - LANES) + 1)
    pick[...] = jnp.where(row == source, 1.0, 0.0).astype(BF16)

    ramp_rows = ramp_even.shape[0]
    block = 128
    shift = half - LANES

    def fill(step, _):
        first = pl.multiple_of(step * block, block)
        row = lax.broadcasted_iota(jnp.int32, (block, LANES), 0) + first
        lane = lax.broadcasted_iota(jnp.int32, (block, LANES), 1)
        twice = 2 * (lane - row + shift)
        ramp_even[pl.ds(first, block), :] = odd_ramp(twice + 1)
        ramp_odd[pl.ds(first, block), :] = odd_ramp(twice - 1)
        return 0

    lax.fori_loop(0, ramp_rows // block, fill, 0)
    volume[...] = jnp.zeros_like(volume)
    foot_wide[...] = jnp.zeros_like(foot_wide)
    for part in (w_even, w_odd):
        part[:, half:] = jnp.zeros((part.shape[0], part.shape[1] - half), BF16)
    foot_copy.wait()

    def view_step(view, _):
        slot = lax.rem(view, 2)
        proj_copy(view, slot).wait()
        for j in range(columns // 256):
            cols = pl.ds(256 * j, 256)
            scaled = (
                proj_buf[slot, :, cols].astype(F32) * weight[pl.ds(view, 1), cols]
            ).astype(BF16)
            parted = jnp.dot(scaled, pick[...], preferred_element_type=F32).astype(BF16)
            w_even[:, pl.ds(LANES * j, LANES)] = parted[:, :LANES]
            w_odd[:, pl.ds(LANES * j, LANES)] = parted[:, LANES:]

        @pl.when(view + 2 < views)
        def _():
            proj_copy(view + 2, slot).start()

        first = start_ref[view]
        base = first // ALIGN
        lead = first - base * ALIGN
        row0 = base * (ALIGN // 2)
        tile = row0 // LANES
        inner = pl.multiple_of(row0 - tile * LANES, 16)
        row0 = pl.multiple_of(row0, 16)
        for part, diag in ((w_even, diag_even), (w_odd, diag_odd)):
            near = part[:, pl.ds(pl.multiple_of(tile * LANES, LANES), diag.shape[0])]
            diag[...] = 0.25 * near.astype(F32).T

        foot_wide[pl.ds(ALIGN, width), :] = foot_buf[view].astype(F32)
        total = None
        for parity, ramp, part, diag in (
            (0, ramp_even, w_odd, diag_even),
            (1, ramp_odd, w_even, diag_odd),
        ):
            acc = diag[pl.ds(inner, window), :]
            for kc in range(half // KC):
                lhs = jnp.concatenate(
                    [
                        ramp[pl.ds(row0 + (shift - KC * kc - LANES * j), window), :]
                        for j in range(KC // LANES)
                    ],
                    axis=1,
                )
                acc += lax.dot_general(
                    lhs, part[:, KC * kc : KC * kc + KC], NT, preferred_element_type=F32
                )
            filtered = acc.astype(BF16)
            foot = foot_wide[pl.ds(ALIGN + parity - lead, window, stride=2), :].astype(BF16)
            term = lax.dot_general(foot, filtered, TN, preferred_element_type=F32)
            total = term if total is None else total + term
        grid_rows[...] = total.T

        place = lax.broadcasted_iota(jnp.int32, (BAND, total.shape[0]), 0)
        for s in range(n_zs):
            rows = grid_rows[pl.ds(offset_ref[view, s], BAND), :]
            volume[s] += jnp.where(place < count_ref[view, s], rows, 0.0)
        return 0

    lax.fori_loop(0, views, view_step, 0)

    share = volume.shape[2] // n_ang
    for s in range(n_zs):
        slab = volume[s]
        for g in range(n_ang):
            piece = slab[:, share * g : share * (g + 1)]
            out_ref[s, g] = jnp.concatenate([piece[: BAND // 2], piece[BAND // 2 :]], axis=1)


def exchange(n_zs, n_ang, send_buf, out_ref, recv_buf, send_sem, recv_sem):
    peers = n_zs * n_ang
    share = out_ref.shape[1]
    my_zs, my_ang = lax.axis_index("zs"), lax.axis_index("ang")
    me = my_zs * n_ang + my_ang
    barrier = pltpu.get_barrier_semaphore()
    for k in range(1, peers):
        peer = lax.rem(me + k, peers)
        pl.semaphore_signal(
            barrier, inc=1,
            device_id={"zs": peer // n_ang, "ang": lax.rem(peer, n_ang)},
            device_id_type=pl.DeviceIdType.MESH,
        )

    pl.semaphore_wait(barrier, peers - 1)
    copies = []
    for k in range(1, peers):
        peer = lax.rem(me + k, peers)
        peer_zs, peer_ang = peer // n_ang, lax.rem(peer, n_ang)
        copy = pltpu.make_async_remote_copy(
            src_ref=send_buf.at[peer_zs, peer_ang],
            dst_ref=recv_buf.at[k],
            send_sem=send_sem.at[k],
            recv_sem=recv_sem.at[k],
            device_id={"zs": peer_zs, "ang": peer_ang},
            device_id_type=pl.DeviceIdType.MESH,
        )
        copy.start()
        copies.append(copy)
    result = send_buf[my_zs, my_ang]
    for k, copy in enumerate(copies):
        copy.wait_recv()
        result += recv_buf[k + 1]
    out_ref[...] = jnp.concatenate([result[:, :share], result[:, share:]], axis=0)
    for copy in copies:
        copy.wait_send()


def shards(n_zs, n_ang, projections, view_angle, band_offset, band_count, fp_start, footprint):
    views, rows, columns = projections.shape
    width, voxels = footprint.shape[1:]
    half = columns // 2
    window = (width + ALIGN) // 2
    ramp_rows = (columns - width) // 2 + (half - LANES) + window
    ramp_rows = -(-ramp_rows // LANES) * LANES
    near = -(-(window + LANES - 16) // LANES) * LANES
    pad = near - width // 2
    peers = n_zs * n_ang
    smem = pl.BlockSpec(memory_space=pltpu.SMEM)
    vmem = pl.BlockSpec(memory_space=pltpu.VMEM)
    hbm = pl.BlockSpec(memory_space=pl.ANY)
    flops = 2 * views * rows * (columns * width // 2 + columns * 256 + width * voxels)
    partial = pl.pallas_call(
        functools.partial(kernel, (n_zs, n_ang, views, columns, width)),
        out_shape=jax.ShapeDtypeStruct((n_zs, n_ang, BAND // 2, voxels), F32),
        in_specs=[smem, smem, smem, vmem, hbm, hbm],
        out_specs=vmem,
        scratch_shapes=[
            pltpu.VMEM((2, rows, columns), BF16),
            pltpu.VMEM((views, width, voxels), BF16),
            pltpu.VMEM((width + 2 * ALIGN, voxels), F32),
            pltpu.VMEM((views, columns), F32),
            pltpu.VMEM((256, 256), BF16),
            pltpu.VMEM((ramp_rows, LANES), BF16),
            pltpu.VMEM((ramp_rows, LANES), BF16),
            pltpu.VMEM((rows, half + pad), BF16),
            pltpu.VMEM((rows, half + pad), BF16),
            pltpu.VMEM((near, rows), F32),
            pltpu.VMEM((near, rows), F32),
            pltpu.VMEM((rows, voxels), F32),
            pltpu.VMEM((n_zs, BAND, voxels), F32),
            pltpu.SemaphoreType.DMA((2,)),
            pltpu.SemaphoreType.DMA,
        ],
        compiler_params=pltpu.CompilerParams(vmem_limit_bytes=48 * 2**20),
        cost_estimate=pl.CostEstimate(
            flops=flops, bytes_accessed=projections.size * 2, transcendentals=0
        ),
        name="filter_backproject",
    )(fp_start, band_offset, band_count, view_angle[:, None], projections, footprint)
    return pl.pallas_call(
        functools.partial(exchange, n_zs, n_ang),
        out_shape=jax.ShapeDtypeStruct((BAND, voxels // n_ang), F32),
        in_specs=[vmem],
        out_specs=vmem,
        scratch_shapes=[
            pltpu.VMEM((peers, BAND // 2, voxels), F32),
            pltpu.SemaphoreType.DMA((peers,)),
            pltpu.SemaphoreType.DMA((peers,)),
        ],
        compiler_params=pltpu.CompilerParams(collective_id=0, has_side_effects=True),
        name="sum_slabs",
    )(partial)


def solution(mesh):
    in_specs = (
        P(("grp", "ang", "zs"), None, None),
        P(("grp", "ang", "zs")),
        P(("grp", "ang", "zs"), None),
        P(("grp", "ang", "zs"), None),
        P(("grp", "ang", "zs")),
        P(("grp", "ang"), None, None),
    )
    out_specs = P(("grp", "zs"), "ang")
    body = functools.partial(shards, mesh.shape["zs"], mesh.shape["ang"])
    return jax.shard_map(body, mesh=mesh, in_specs=in_specs, out_specs=out_specs, check_vma=False)
```

time: 344 us -> 39.8 us (0.12)
  matrix products: 153 us -> 0 us
  blocking collectives: 100 us -> 0 us
  local copies, waits for them, and re-layouts: 41 us -> 4.72 us
  Pallas kernels: 0 us -> 34.7 us
  other arithmetic: 19.4 us -> 0 us
  between operations: 13.4 us -> 0.03 us
  loops' own time: 9.86 us -> 0 us
  waiting for transfers between devices: 6.53 us -> 0 us
    dot_general x9 -> x0, matrix products: 153 us -> none  [the longest x8 142 us: filter_view(): jnp.dot(weighted, kernel, preferred_element_type=jnp.float32)]
    all_to_all x1 -> x0, blocking collectives: 100 us -> none  [shards(): lax.all_to_all(bands, 'zs', split_axis=0, concat_axis=0, tiled=True)]
    pallas_call x0 -> x2, Pallas kernels: none -> 34.7 us  [the longest x1 23.8 us: shards(): pl.pallas_call(functools.partial(kernel, (n_zs, n_ang, views, columns, wi...]
    dynamic_slice x16 -> x0, local copies, waits for them, and re-layouts: 20.3 us -> none  [shards(): filtered = lax.map(filter_view, (projections, view_angle, fp_start))]
    gather x2 -> x0, local copies, waits for them, and re-layouts: 12.6 us -> none  [cut_band(): lax.dynamic_slice_in_dim(view_filtered, first_row, band_rows, 0)]
    another operation x1 -> x0, loops' own time: 9.86 us -> none  [shards(): filtered = lax.map(filter_view, (projections, view_angle, fp_start))]
    select_n x1 -> x0, other arithmetic: 8.06 us -> none  [cut_band(): return jnp.where(keep_rows[:, None], rows_taken, jnp.zeros_like(rows_taken))]
    unnamed x2 -> x0, waiting for transfers between devices: 6.53 us -> none
  transfers between devices with their start and end apart: 1 -> 0, of which waited for: 1 -> 0; matrix products, arithmetic and copies ran while one was open for 0% -> 0% of each run, Pallas kernels for 0% -> 0%
where the time goes in v1:
time: 39.8 us; the launch traced here: 39.4 us
  Pallas kernels  34.7 us (87%)
  local copies, waits for them, and re-layouts  4.72 us (12%)
    pallas_call x1, Pallas kernels, shards(): pl.pallas_call(functools.partial(kernel, (n_zs, n_ang, views, columns, wi...  23.8 us
    pallas_call x1, Pallas kernels, shards(): pl.pallas_call(functools.partial(exchange, n_zs, n_ang), out_shape=jax.Sh...  10.9 us
    unnamed x9, local copies, waits for them, and re-layouts  3.99 us

profile of v1, /device:TPU:0, one launch (start us, length us, event | category | flops | bytes accessed | tf_op | source)
XLA Modules:
  0.0 39.4 jit_solution(17796016258771536530)
XLA Ops:
  0.0 0.7 %copy.7.angle_ref = f32[8,1]{1,0:T(8,128)S(1)} copy(f32[8,1]{0,1:T(1,128)} %bitcast.1) | data formatting | bytes 64 | tf_op jit(solution)/shard_map/broadcast_in_dim | solution.py:236
  0.7 0.0 copy-start.1
  0.7 0.7 %copy-done.1 = s32[8,8]{1,0:T(8,128)S(1)} copy-done((s32[8,8]{1,0:T(8,128)S(1)}, s32[8,8]{1,0:T(8,128)}, u32[]{:S(2)}) %copy-start.1) | copy-done | bytes 280
  1.4 0.0 copy-start.2
  1.4 0.7 %copy-done.2 = s32[8,8]{1,0:T(8,128)S(1)} copy-done((s32[8,8]{1,0:T(8,128)S(1)}, s32[8,8]{1,0:T(8,128)}, u32[]{:S(2)}) %copy-start.2) | copy-done | bytes 280
  2.1 0.0 copy-start.3
  2.1 0.7 %copy-done.3 = s32[8]{0:T(128)S(1)} copy-done((s32[8]{0:T(128)S(1)}, s32[8]{0:T(128)}, u32[]{:S(2)}) %copy-start.3) | copy-done | bytes 56
  2.8 23.8 %filter_backproject.1.send_buf = f32[8,2,16,128]{3,2,1,0:T(8,128)S(1)} custom-call(s32[8]{0:T(128)S(1)} %copy-done.3, s32[8,8]{1,0:T(8,128)S(1)} %copy-done.1, s32[8,8]{1,0:T(8,128)S(1)} %copy-done.2, f32[8,1]{1,0:T(8,128)S(1)} %copy.7.angle_ref, bf16[8,256,4096]{2,1,0:T(8,128)(2,1)} %proj_ref.1, bf16[64,1024,128]{2,1,0:T(8,128)(2,1)} %foot_ref.1), custom_call_target="tpu_custom_call" | custom-call | flops 13421772800 | bytes 16777216 | tf_op jit(solution)/shard_map/filter_backproject/pallas_call | solution.py:209
  26.6 0.0 copy-start
  26.6 0.6 %copy-done = f32[8,2,16,128]{3,2,1,0:T(8,128)} copy-done((f32[8,2,16,128]{3,2,1,0:T(8,128)}, f32[8,2,16,128]{3,2,1,0:T(8,128)S(1)}, u32[]{:S(2)}) %copy-start) | copy-done | bytes 131096
  27.2 10.9 %sum_slabs.1 = f32[32,64]{1,0:T(8,128)} custom-call(f32[8,2,16,128]{3,2,1,0:T(8,128)} %copy-done), custom_call_target="tpu_custom_call" | custom-call | tf_op jit(solution)/shard_map/sum_slabs/pallas_call | solution.py:237
  38.1 1.3 %copy.9 = f32[32,64]{1,0:T(8,128)} copy(f32[32,64]{1,0:T(8,128)} %sum_slabs.1) | data formatting | bytes 16384
Async XLA Ops:
  0.7 0.7 %copy-start.1 = (s32[8,8]{1,0:T(8,128)S(1)}, s32[8,8]{1,0:T(8,128)}, u32[]{:S(2)}) copy-start(s32[8,8]{1,0:T(8,128)} %offset_ref.1) | copy-start | bytes 772
  1.4 0.7 %copy-start.2 = (s32[8,8]{1,0:T(8,128)S(1)}, s32[8,8]{1,0:T(8,128)}, u32[]{:S(2)}) copy-start(s32[8,8]{1,0:T(8,128)} %count_ref.1) | copy-start | bytes 772
  2.1 0.7 %copy-start.3 = (s32[8]{0:T(128)S(1)}, s32[8]{0:T(128)}, u32[]{:S(2)}) copy-start(s32[8]{0:T(128)} %start_ref.1) | copy-start | bytes 100
  26.6 0.6 %copy-start = (f32[8,2,16,128]{3,2,1,0:T(8,128)}, f32[8,2,16,128]{3,2,1,0:T(8,128)S(1)}, u32[]{:S(2)}) copy-start(f32[8,2,16,128]{3,2,1,0:T(8,128)S(1)} %filter_backproject.1.send_buf) | copy-start | bytes 393220

commit v2 on v1

--- a/solution.py
+++ b/solution.py
@@ -12,7 +12,7 @@
 FAN_HALF = 0.5
 LANES = 128
 ALIGN = 32
-KC = 512
+KC = 2048
 F32 = jnp.float32
 BF16 = jnp.bfloat16
 NT = (((1,), (1,)), ((), ()))
@@ -41,9 +41,10 @@
 
 def kernel(
     sizes,
-    start_ref, offset_ref, count_ref, angle_ref, proj_ref, foot_ref, out_ref,
+    start_hbm, offset_hbm, count_hbm, angle_hbm, proj_ref, foot_ref, out_ref,
+    start_ref, offset_ref, count_ref, angle_ref,
     proj_buf, foot_buf, foot_wide, weight, pick, ramp_even, ramp_odd,
-    w_even, w_odd, diag_even, diag_odd, grid_rows, volume, proj_sem, foot_sem,
+    w_even_0, w_odd_0, w_even_1, w_odd_1, diag_even, diag_odd, grid_rows, volume, proj_sem, foot_sem, small_sem,
 ):
     n_zs, n_ang, views, columns, width = sizes
     half = columns // 2
@@ -53,14 +54,21 @@
     def proj_copy(view, slot):
         return pltpu.make_async_copy(proj_ref.at[view], proj_buf.at[slot], proj_sem.at[slot])
 
+    small = [
+        pltpu.make_async_copy(source, target, small_sem.at[i])
+        for i, (source, target) in enumerate(
+            ((angle_hbm, angle_ref), (start_hbm, start_ref),
+             (offset_hbm, offset_ref), (count_hbm, count_ref))
+        )
+    ]
+    for copy in small:
+        copy.start()
     proj_copy(0, 0).start()
     proj_copy(1, 1).start()
     foot_copy = pltpu.make_async_copy(
         foot_ref.at[pl.ds(my_zs * views, views)], foot_buf, foot_sem
     )
     foot_copy.start()
-
-    weight[...] = fan_weight(angle_ref[...], columns)
 
     row = lax.broadcasted_iota(jnp.int32, (256, 256), 0)
     col = lax.broadcasted_iota(jnp.int32, (256, 256), 1)
@@ -83,25 +91,31 @@
     lax.fori_loop(0, ramp_rows // block, fill, 0)
     volume[...] = jnp.zeros_like(volume)
     foot_wide[...] = jnp.zeros_like(foot_wide)
-    for part in (w_even, w_odd):
+    for part in (w_even_0, w_odd_0, w_even_1, w_odd_1):
         part[:, half:] = jnp.zeros((part.shape[0], part.shape[1] - half), BF16)
+    for copy in small:
+        copy.wait()
+    which = lax.broadcasted_iota(jnp.int32, (views, 1), 0)
+    beta = jnp.zeros((views, 1), F32)
+    for a in range(views):
+        beta = jnp.where(which == a, angle_ref[a], beta)
+    weight[...] = fan_weight(beta, columns)
     foot_copy.wait()
 
-    def view_step(view, _):
-        slot = lax.rem(view, 2)
-        proj_copy(view, slot).wait()
-        for j in range(columns // 256):
-            cols = pl.ds(256 * j, 256)
-            scaled = (
-                proj_buf[slot, :, cols].astype(F32) * weight[pl.ds(view, 1), cols]
-            ).astype(BF16)
-            parted = jnp.dot(scaled, pick[...], preferred_element_type=F32).astype(BF16)
-            w_even[:, pl.ds(LANES * j, LANES)] = parted[:, :LANES]
-            w_odd[:, pl.ds(LANES * j, LANES)] = parted[:, LANES:]
-
-        @pl.when(view + 2 < views)
-        def _():
-            proj_copy(view + 2, slot).start()
+    def part_block(view, slot, j, w_even, w_odd):
+        cols = pl.ds(256 * j, 256)
+        scaled = (
+            proj_buf[slot, :, cols].astype(F32) * weight[pl.ds(view, 1), cols]
+        ).astype(BF16)
+        parted = jnp.dot(scaled, pick[...], preferred_element_type=F32).astype(BF16)
+        w_even[:, pl.ds(LANES * j, LANES)] = parted[:, :LANES]
+        w_odd[:, pl.ds(LANES * j, LANES)] = parted[:, LANES:]
+
+    def view_step(view, now, later):
+        following = jnp.minimum(view + 1, views - 1)
+        blocks = columns // 256
+        chunks = 2 * (half // KC)
+        emitted = 0
 
         first = start_ref[view]
         base = first // ALIGN
@@ -110,6 +124,7 @@
         tile = row0 // LANES
         inner = pl.multiple_of(row0 - tile * LANES, 16)
         row0 = pl.multiple_of(row0, 16)
+        w_even, w_odd = now
         for part, diag in ((w_even, diag_even), (w_odd, diag_odd)):
             near = part[:, pl.ds(pl.multiple_of(tile * LANES, LANES), diag.shape[0])]
             diag[...] = 0.25 * near.astype(F32).T
@@ -132,6 +147,9 @@
                 acc += lax.dot_general(
                     lhs, part[:, KC * kc : KC * kc + KC], NT, preferred_element_type=F32
                 )
+                for j in range(blocks // chunks):
+                    part_block(following, (now_slot[0] + 1) % 2, emitted, *later)
+                    emitted += 1
             filtered = acc.astype(BF16)
             foot = foot_wide[pl.ds(ALIGN + parity - lead, window, stride=2), :].astype(BF16)
             term = lax.dot_general(foot, filtered, TN, preferred_element_type=F32)
@@ -142,54 +160,96 @@
         for s in range(n_zs):
             rows = grid_rows[pl.ds(offset_ref[view, s], BAND), :]
             volume[s] += jnp.where(place < count_ref[view, s], rows, 0.0)
+
+    now_slot = [0]
+    ring = ((w_even_0, w_odd_0), (w_even_1, w_odd_1))
+    proj_copy(0, 0).wait()
+    for j in range(columns // 256):
+        part_block(0, 0, j, *ring[0])
+
+    @pl.when(2 < views)
+    def _():
+        proj_copy(2, 0).start()
+
+    def pair_step(pair, _):
+        for slot in range(2):
+            view = 2 * pair + slot
+            other = 1 - slot
+
+            @pl.when(view + 1 < views)
+            def _():
+                proj_copy(view + 1, other).wait()
+
+            now_slot[0] = slot
+            view_step(view, ring[slot], ring[other])
+
+            @pl.when(view + 3 < views)
+            def _():
+                proj_copy(view + 3, other).start()
         return 0
 
-    lax.fori_loop(0, views, view_step, 0)
+    lax.fori_loop(0, views // 2, pair_step, 0)
 
     share = volume.shape[2] // n_ang
     for s in range(n_zs):
         slab = volume[s]
         for g in range(n_ang):
             piece = slab[:, share * g : share * (g + 1)]
-            out_ref[s, g] = jnp.concatenate([piece[: BAND // 2], piece[BAND // 2 :]], axis=1)
-
-
-def exchange(n_zs, n_ang, send_buf, out_ref, recv_buf, send_sem, recv_sem):
-    peers = n_zs * n_ang
+            out_ref[g, s] = jnp.concatenate([piece[: BAND // 2], piece[BAND // 2 :]], axis=1)
+
+
+def greet(peers):
+    barrier = pltpu.get_barrier_semaphore()
+    for peer in peers:
+        pl.semaphore_signal(
+            barrier, inc=1, device_id=peer, device_id_type=pl.DeviceIdType.MESH
+        )
+    return barrier
+
+
+def partners(n_zs, n_ang):
+    my_zs, my_ang = lax.axis_index("zs"), lax.axis_index("ang")
+    near = [lax.rem(my_ang + k, n_ang) for k in range(1, n_ang)]
+    far = [lax.rem(my_zs + k, n_zs) for k in range(1, n_zs)]
+    ids = [{"zs": my_zs, "ang": g} for g in near] + [{"zs": z, "ang": my_ang} for z in far]
+    return near, far, ids
+
+
+def finish(n_zs, n_ang, barrier, send_buf, out_ref, near_buf, sum_buf, far_buf, send_sem, recv_sem):
     share = out_ref.shape[1]
     my_zs, my_ang = lax.axis_index("zs"), lax.axis_index("ang")
-    me = my_zs * n_ang + my_ang
-    barrier = pltpu.get_barrier_semaphore()
-    for k in range(1, peers):
-        peer = lax.rem(me + k, peers)
-        pl.semaphore_signal(
-            barrier, inc=1,
-            device_id={"zs": peer // n_ang, "ang": lax.rem(peer, n_ang)},
-            device_id_type=pl.DeviceIdType.MESH,
-        )
-
-    pl.semaphore_wait(barrier, peers - 1)
-    copies = []
-    for k in range(1, peers):
-        peer = lax.rem(me + k, peers)
-        peer_zs, peer_ang = peer // n_ang, lax.rem(peer, n_ang)
+    near, far, ids = partners(n_zs, n_ang)
+    pl.semaphore_wait(barrier, len(ids))
+
+    def start(i, source, target):
         copy = pltpu.make_async_remote_copy(
-            src_ref=send_buf.at[peer_zs, peer_ang],
-            dst_ref=recv_buf.at[k],
-            send_sem=send_sem.at[k],
-            recv_sem=recv_sem.at[k],
-            device_id={"zs": peer_zs, "ang": peer_ang},
-            device_id_type=pl.DeviceIdType.MESH,
+            src_ref=source, dst_ref=target,
+            send_sem=send_sem.at[i], recv_sem=recv_sem.at[i],
+            device_id=ids[i], device_id_type=pl.DeviceIdType.MESH,
         )
         copy.start()
-        copies.append(copy)
-    result = send_buf[my_zs, my_ang]
-    for k, copy in enumerate(copies):
+        return copy
+
+    copies = [start(i, send_buf.at[g], near_buf.at[i]) for i, g in enumerate(near)]
+    total = send_buf[my_ang]
+    for i, copy in enumerate(copies):
         copy.wait_recv()
-        result += recv_buf[k + 1]
+        total += near_buf[i]
+    sum_buf[...] = total
+    for i, z in enumerate(far):
+        copies.append(start(len(near) + i, sum_buf.at[z], far_buf.at[i]))
+    result = sum_buf[my_zs]
+    for i, copy in enumerate(copies[len(near):]):
+        copy.wait_recv()
+        result += far_buf[i]
     out_ref[...] = jnp.concatenate([result[:, :share], result[:, share:]], axis=0)
     for copy in copies:
         copy.wait_send()
+
+
+def exchange(n_zs, n_ang, send_buf, out_ref, *scratch):
+    barrier = greet(partners(n_zs, n_ang)[2])
+    finish(n_zs, n_ang, barrier, send_buf, out_ref, *scratch)
 
 
 def shards(n_zs, n_ang, projections, view_angle, band_offset, band_count, fp_start, footprint):
@@ -201,17 +261,20 @@
     ramp_rows = -(-ramp_rows // LANES) * LANES
     near = -(-(window + LANES - 16) // LANES) * LANES
     pad = near - width // 2
-    peers = n_zs * n_ang
-    smem = pl.BlockSpec(memory_space=pltpu.SMEM)
+    peers = n_zs + n_ang - 2
     vmem = pl.BlockSpec(memory_space=pltpu.VMEM)
     hbm = pl.BlockSpec(memory_space=pl.ANY)
     flops = 2 * views * rows * (columns * width // 2 + columns * 256 + width * voxels)
     partial = pl.pallas_call(
         functools.partial(kernel, (n_zs, n_ang, views, columns, width)),
-        out_shape=jax.ShapeDtypeStruct((n_zs, n_ang, BAND // 2, voxels), F32),
-        in_specs=[smem, smem, smem, vmem, hbm, hbm],
+        out_shape=jax.ShapeDtypeStruct((n_ang, n_zs, BAND // 2, voxels), F32),
+        in_specs=[hbm] * 6,
         out_specs=vmem,
         scratch_shapes=[
+            pltpu.SMEM(fp_start.shape, jnp.int32),
+            pltpu.SMEM(band_offset.shape, jnp.int32),
+            pltpu.SMEM(band_count.shape, jnp.int32),
+            pltpu.SMEM(view_angle.shape, F32),
             pltpu.VMEM((2, rows, columns), BF16),
             pltpu.VMEM((views, width, voxels), BF16),
             pltpu.VMEM((width + 2 * ALIGN, voxels), F32),
@@ -221,26 +284,31 @@
             pltpu.VMEM((ramp_rows, LANES), BF16),
             pltpu.VMEM((rows, half + pad), BF16),
             pltpu.VMEM((rows, half + pad), BF16),
+            pltpu.VMEM((rows, half + pad), BF16),
+            pltpu.VMEM((rows, half + pad), BF16),
             pltpu.VMEM((near, rows), F32),
             pltpu.VMEM((near, rows), F32),
             pltpu.VMEM((rows, voxels), F32),
             pltpu.VMEM((n_zs, BAND, voxels), F32),
             pltpu.SemaphoreType.DMA((2,)),
             pltpu.SemaphoreType.DMA,
+            pltpu.SemaphoreType.DMA((4,)),
         ],
-        compiler_params=pltpu.CompilerParams(vmem_limit_bytes=48 * 2**20),
+        compiler_params=pltpu.CompilerParams(vmem_limit_bytes=63 * 2**20),
         cost_estimate=pl.CostEstimate(
             flops=flops, bytes_accessed=projections.size * 2, transcendentals=0
         ),
         name="filter_backproject",
-    )(fp_start, band_offset, band_count, view_angle[:, None], projections, footprint)
+    )(fp_start, band_offset, band_count, view_angle, projections, footprint)
     return pl.pallas_call(
         functools.partial(exchange, n_zs, n_ang),
         out_shape=jax.ShapeDtypeStruct((BAND, voxels // n_ang), F32),
         in_specs=[vmem],
         out_specs=vmem,
         scratch_shapes=[
-            pltpu.VMEM((peers, BAND // 2, voxels), F32),
+            pltpu.VMEM((n_ang - 1, n_zs, BAND // 2, voxels), F32),
+            pltpu.VMEM((n_zs, BAND // 2, voxels), F32),
+            pltpu.VMEM((n_zs - 1, BAND // 2, voxels), F32),
             pltpu.SemaphoreType.DMA((peers,)),
             pltpu.SemaphoreType.DMA((peers,)),
         ],

time: 39.8 us -> 35.1 us (0.88)
  local copies, waits for them, and re-layouts: 4.72 us -> 1.32 us
  Pallas kernels: 34.7 us -> 33.6 us
    unnamed x9 -> x1, local copies, waits for them, and re-layouts: 3.99 us -> 1.32 us
    pallas_call x1, Pallas kernels: 23.8 us -> 22.6 us  [shards(): pl.pallas_call(functools.partial(kernel, (n_zs, n_ang, views, columns, wi...]
    broadcast_in_dim x1 -> x0, local copies, waits for them, and re-layouts: 0.73 us -> none  [shards(): view_angle[:, None]]
where the time goes in v2:
time: 35.1 us; the launch traced here: 35 us
  Pallas kernels  33.6 us (96%)
  local copies, waits for them, and re-layouts  1.32 us (4%)
    pallas_call x1, Pallas kernels, shards(): pl.pallas_call(functools.partial(kernel, (n_zs, n_ang, views, columns, wi...  22.6 us
    pallas_call x1, Pallas kernels, shards(): pl.pallas_call(functools.partial(exchange, n_zs, n_ang), out_shape=jax.Sh...  11.1 us
    unnamed x1, local copies, waits for them, and re-layouts  1.32 us

profile of v2, /device:TPU:0, one launch (start us, length us, event | category | flops | bytes accessed | tf_op | source)
XLA Modules:
  0.0 35.0 jit_solution(3773735270933888202)
XLA Ops:
  0.0 22.6 %filter_backproject.1.send_buf = f32[2,8,16,128]{3,2,1,0:T(8,128)} custom-call(s32[8]{0:T(128)} %start_hbm.1, s32[8,8]{1,0:T(8,128)} %offset_hbm.1, s32[8,8]{1,0:T(8,128)} %count_hbm.1, f32[8]{0:T(128)} %angle_hbm.1, bf16[8,256,4096]{2,1,0:T(8,128)(2,1)} %proj_ref.1, bf16[64,1024,128]{2,1,0:T(8,128)(2,1)} %foot_ref.1), custom_call_target="tpu_custom_call" | custom-call | flops 13421772800 | bytes 16777216 | tf_op jit(solution)/shard_map/filter_backproject/pallas_call | solution.py:268
  22.6 11.1 %sum_slabs.1 = f32[32,64]{1,0:T(8,128)} custom-call(f32[2,8,16,128]{3,2,1,0:T(8,128)} %filter_backproject.1.send_buf), custom_call_target="tpu_custom_call" | custom-call | tf_op jit(solution)/shard_map/sum_slabs/pallas_call | solution.py:303
  33.6 1.3 %copy.8 = f32[32,64]{1,0:T(8,128)} copy(f32[32,64]{1,0:T(8,128)} %sum_slabs.1) | data formatting | bytes 16384
